TPU v7x, 128 devices: a whole 4x4x4 slice. The times are simulated.
128 devices in a mesh: vrow: 8 (over z, core), ecol: 16 (over x, y).
Axes of the slice: x: 4, y: 4, z: 4, core: 2. Of those that a mesh axis runs over, the one named last changes fastest.
Arguments:
- features: bfloat16 [32768, 256], P(('vrow', 'ecol')), may hold values from -6 to 6
- grad_out: bfloat16 [32768, 256], P(('vrow', 'ecol')), may hold values from -6 to 6
- theta: bfloat16 [256, 256], replicated, may hold values from -0.375 to 0.375
- tile_values: bfloat16 [32768, 128, 128], P(('vrow', 'ecol')), may hold values from -0.09375 to 0.09375
- tile_rows: int32 [32768], P(('vrow', 'ecol')), may hold values from 0 to 31
- tile_cols: int32 [32768], P(('vrow', 'ecol')), may hold values from 0 to 23
- tile_count: int32 [128], P(('vrow', 'ecol')), may hold values from 1 to 256, 12288 in all
- vertex_degree: int32 [32768], P(('vrow', 'ecol')), may hold values from 1 to 8
- edge_weight: float32 [16, 3072], P('ecol', 'vrow'), may hold values from 0.25 to 4
- edge_degree: int32 [16, 3072], P('ecol', 'vrow'), may hold values from 1 to 8
Outputs:
- out_y: bfloat16 [32768, 256], P(('vrow', 'ecol'))
- grad_x: bfloat16 [32768, 256], P(('vrow', 'ecol'))
- grad_theta: float32 [256, 256], replicated
- grad_w: float32 [16, 3072], P('ecol', 'vrow')
Inputs may be any that keep to these rules, and one draw needn't show every extreme that they name: `tile_count`: live tile slots of a device; some device has all 256 live.
All inputs are finite; a program needn't handle non-finite values.
Results may differ from a plain program's by a relative error of at most 0.0055.
Values may be sent and summed in bfloat16 or wider, within the bound.
A program may use at most 128 MiB of HBM per device.

v0:
```python
import math

import jax
import jax.numpy as jnp
from jax import lax
from jax.sharding import PartitionSpec as P

EB = 24


def accumulate(values, rows, cols, live, panels, out_blocks, forward):
    slots = values.shape[0]
    step = math.gcd(32, slots)
    tile = values.shape[1]
    width = panels.shape[-1]
    blocks = (live + step - 1) // step

    def turn(index, total):
        first = index * step
        vals = lax.dynamic_slice_in_dim(values, first, step, 0)
        rws = lax.dynamic_slice_in_dim(rows, first, step, 0)
        cls = lax.dynamic_slice_in_dim(cols, first, step, 0)
        valid = first + jnp.arange(step, dtype=jnp.int32) < live
        if forward:
            picked = panels[rws]
            product = jnp.einsum("tvc,tvw->tcw", vals, picked, preferred_element_type=jnp.float32)
            target = cls
        else:
            picked = panels[cls]
            product = jnp.einsum("tvc,tcw->tvw", vals, picked, preferred_element_type=jnp.float32)
            target = rws
        masked = jnp.where(valid[:, None, None], product, 0.0)
        return total.at[target].add(masked)

    init = jnp.zeros((out_blocks, tile, width), jnp.float32)
    return lax.fori_loop(0, blocks, turn, init)


def shards(
    features,
    grad_out,
    theta,
    tile_values,
    tile_rows,
    tile_cols,
    tile_count,
    vertex_degree,
    edge_weight,
    edge_degree,
):
    live = tile_count[0]
    tile = tile_values.shape[1]
    vertex_scale = 1.0 / jnp.sqrt(vertex_degree.astype(jnp.float32))
    degree_edge = edge_degree.reshape(-1).astype(jnp.float32)
    coefs = edge_weight.reshape(-1) / degree_edge
    own_edges = coefs.shape[0]
    projected = jnp.dot(features, theta, preferred_element_type=jnp.float32)
    scaled_z = (projected * vertex_scale[:, None]).astype(jnp.bfloat16)
    scaled_g = (grad_out.astype(jnp.float32) * vertex_scale[:, None]).astype(jnp.bfloat16)

    def sweep(stacked):
        width = stacked.shape[1]
        gathered = lax.all_gather(stacked, "ecol", axis=0, tiled=True)
        vertex_blocks = gathered.shape[0] // tile
        panels = gathered.reshape(vertex_blocks, tile, width)
        partial_value = accumulate(
            tile_values, tile_rows, tile_cols, live, panels, EB, True
        ).reshape(EB * tile, width)
        own = lax.psum_scatter(partial_value, "vrow", scatter_dimension=0, tiled=True)
        scaled = (own * coefs[:, None]).astype(jnp.bfloat16)
        column = lax.all_gather(scaled, "vrow", axis=0, tiled=True)
        edge_panels = column.reshape(EB, tile, width)
        back = accumulate(
            tile_values, tile_rows, tile_cols, live, edge_panels, vertex_blocks, False
        )
        vertex_sum = lax.psum_scatter(
            back.reshape(vertex_blocks * tile, width), "ecol", scatter_dimension=0, tiled=True
        )
        return (own, vertex_sum)

    edge_z, vertex_z = sweep(scaled_z)
    edge_g, vertex_g = sweep(scaled_g)
    out_y = (vertex_z * vertex_scale[:, None]).astype(jnp.bfloat16)
    grad_z = (vertex_g * vertex_scale[:, None]).astype(jnp.bfloat16)
    grad_x = lax.dot_general(
        grad_z, theta, (((1,), (1,)), ((), ())), preferred_element_type=jnp.float32
    ).astype(jnp.bfloat16)
    local_theta = lax.dot_general(
        features, grad_z, (((0,), (0,)), ((), ())), preferred_element_type=jnp.float32
    )
    grad_theta = lax.psum(local_theta, ("vrow", "ecol"))
    grad_w = (jnp.sum(edge_z * edge_g, axis=1) / degree_edge).reshape(1, own_edges)
    return (out_y, grad_x, grad_theta, grad_w)


def solution(mesh):
    in_specs = (
        P(("vrow", "ecol"), None),
        P(("vrow", "ecol"), None),
        P(),
        P(("vrow", "ecol"), None, None),
        P(("vrow", "ecol")),
        P(("vrow", "ecol")),
        P(("vrow", "ecol")),
        P(("vrow", "ecol")),
        P("ecol", "vrow"),
        P("ecol", "vrow"),
    )
    out_specs = (P(("vrow", "ecol"), None), P(("vrow", "ecol"), None), P(), P("ecol", "vrow"))
    return jax.shard_map(shards, mesh=mesh, in_specs=in_specs, out_specs=out_specs, check_vma=False)
```

profile of v0, /device:TPU:0, one launch (start us, length us, event | category | flops | bytes accessed | tf_op | source)
XLA Modules:
  0.0 870.9 jit_solution(4653439713540070082)
XLA Ops:
  7.2 0.7 convert_rsqrt_fusion
  7.9 0.1 copy-done
  8.1 1.7 fusion.8
  9.9 1.7 multiply_convert_fusion.3
  12.3 12.0 %copy.14 = bf16[256,128,128]{1,2,0:T(8,128)(2,1)} copy(bf16[256,128,128]{2,1,0:T(8,128)(2,1)} %param.21) | data formatting | bytes 16777216 | tf_op jit(solution)/shard_map/while | solution.py:36
  24.3 33.7 %all-gather.5.cloned.1.call-done = bf16[4096,256]{1,0:T(8,128)(2,1)} async-done(((bf16[256,256]{1,0:T(8,128)(2,1)}), bf16[4096,256]{1,0:T(8,128)(2,1)}) %all-gather.5.cloned.1.call-update) | async-done | bytes 2097168 | tf_op jit(solution)/shard_map/all_gather | solution.py:63
  58.0 0.3 broadcast.77.clone
  58.4 15.4 %while.40 = (s32[]{:T(128)}, f32[24,128,256]{2,1,0:T(8,128)S(1)}, s32[]{:T(128)}, s32[256]{0:T(256)S(1)}, s32[]{:T(128)}, /*index=5*/bf16[256,128,128]{1,2,0:T(8...) while((s32[]{:T(128)}, f32[24,128,256]{2,1,0:T(8,128)S(1)}, ...), condition=%wide.region_2.3_spmd, body=%wide.region_0.2_spmd.sunk | while | flops 270533888 | bytes 24122484 | solution.py:36
  58.5 3.6 gather_fusion
  62.1 0.7 add_compare_fusion.8
  62.7 4.6 convolution_select_fusion.8
  67.3 6.5 scatter_fusion
  73.8 1.6 copy-done.1
  75.5 29.4 %all-gather.9.cloned.1.call-done = bf16[4096,256]{1,0:T(8,128)(2,1)} async-done(((bf16[256,256]{1,0:T(8,128)(2,1)}), bf16[4096,256]{1,0:T(8,128)(2,1)}) %all-gather.9.cloned.1.call-update) | async-done | bytes 2097168 | tf_op jit(solution)/shard_map/all_gather | solution.py:63
  104.9 0.3 broadcast.77.clone.1
  105.3 15.4 %while.42 = (s32[]{:T(128)}, f32[24,128,256]{2,1,0:T(8,128)S(1)}, s32[]{:T(128)}, s32[256]{0:T(256)S(1)}, s32[]{:T(128)}, /*index=5*/bf16[256,128,128]{1,2,0:T(8...) while((s32[]{:T(128)}, f32[24,128,256]{2,1,0:T(8,128)S(1)}, ...), condition=%wide.region_10.11_spmd, body=%wide.region_8.10_spmd.sunk | while | flops 270533888 | bytes 24122484 | solution.py:36
  105.3 0.1 compare_select_fusion.14
  105.4 3.6 gather_fusion.2
  109.0 0.7 add_compare_fusion.10
  109.7 4.6 convolution_select_fusion.10
  114.2 6.5 scatter_fusion.2
  120.8 1.6 copy-done.2
  122.5 96.3 %reduce-scatter.5.cloned.1.call-done = f32[384,256]{1,0:T(8,128)} async-done(((f32[3072,256]{1,0:T(8,128)}), f32[384,256]{1,0:T(8,128)}) %reduce-scatter.5.cloned.1.call-update) | async-done | bytes 393232 | tf_op jit(solution)/shard_map/reduce_scatter | solution.py:69
  218.8 125.8 %reduce-scatter.9.cloned.1.call-done = f32[384,256]{1,0:T(8,128)} async-done(((f32[3072,256]{1,0:T(8,128)}), f32[384,256]{1,0:T(8,128)}) %reduce-scatter.9.cloned.1.call-update) | async-done | bytes 393232 | tf_op jit(solution)/shard_map/reduce_scatter | solution.py:69
  344.6 2.0 multiply_reduce_fusion
  346.6 0.5 all-gather.7.cloned.1.call-update
  347.2 22.7 %all-gather.11.cloned.1.call-done = bf16[3072,256]{1,0:T(8,128)(2,1)} async-done(((bf16[384,256]{1,0:T(8,128)(2,1)}), bf16[3072,256]{1,0:T(8,128)(2,1)}) %all-gather.11.cloned.1.call-update) | async-done | bytes 1572880 | tf_op jit(solution)/shard_map/all_gather | solution.py:71
  369.9 2.5 broadcast.76.clone.1
  372.4 16.5 %while.43 = (s32[]{:T(128)}, f32[32,128,256]{2,1,0:T(8,128)}, s32[]{:T(128)}, s32[256]{0:T(256)S(1)}, s32[]{:T(128)}, /*index=5*/bf16[256,128,128]{2,1,0:T(8,128...) while((s32[]{:T(128)}, f32[32,128,256]{2,1,0:T(8,128)}, ...), condition=%wide.region_14.15_spmd, body=%wide.region_12.14_spmd.sunk | while | flops 270533888 | bytes 24122484 | solution.py:36
  372.5 2.1 gather_fusion.3
  374.6 0.7 add_compare_fusion.11
  375.2 3.9 convolution_select_fusion.11
  379.1 9.8 %scatter_fusion.3 = f32[32,128,256]{2,1,0:T(8,128)} fusion(f32[32,128,256]{2,1,0:T(8,128)} %get-tuple-element.612, s32[32]{0:T(128)S(1)} %get-tuple-element.489, f32[32,128,256]{2,1,0:T(8,128)} %convolution_select_fusion.11), kind=kCustom, calls=%fused_computation.7.clone.1 | custom fusion | flops 1048576 | bytes 12583040 | tf_op jit(solution)/shard_map/while/body/scatter-add | solution.py:33
  389.0 7.1 all-gather.7.cloned.1.call-done
  396.1 2.5 broadcast.76.clone
  398.6 16.5 %while.41 = (s32[]{:T(128)}, f32[32,128,256]{2,1,0:T(8,128)}, s32[]{:T(128)}, s32[256]{0:T(256)S(1)}, s32[]{:T(128)}, /*index=5*/bf16[256,128,128]{2,1,0:T(8,128...) while((s32[]{:T(128)}, f32[32,128,256]{2,1,0:T(8,128)}, ...), condition=%wide.region_6.7_spmd, body=%wide.region_4.6_spmd.sunk | while | flops 270533888 | bytes 24122484 | solution.py:36
  398.6 2.1 gather_fusion.1
  400.7 0.7 add_compare_fusion.9
  401.4 3.9 convolution_select_fusion.9
  405.3 9.8 %scatter_fusion.1 = f32[32,128,256]{2,1,0:T(8,128)} fusion(f32[32,128,256]{2,1,0:T(8,128)} %get-tuple-element.576, s32[32]{0:T(128)S(1)} %get-tuple-element.469, f32[32,128,256]{2,1,0:T(8,128)} %convolution_select_fusion.9), kind=kCustom, calls=%fused_computation.5.clone.1 | custom fusion | flops 1048576 | bytes 12583040 | tf_op jit(solution)/shard_map/while/body/scatter-add | solution.py:33
  415.2 0.6 reshape_divide_fusion
  415.7 165.5 %reduce-scatter.11.cloned.1.call-done = f32[256,256]{1,0:T(8,128)} async-done(((f32[4096,256]{1,0:T(8,128)}), f32[256,256]{1,0:T(8,128)}) %reduce-scatter.11.cloned.1.call-update) | async-done | bytes 262160 | tf_op jit(solution)/shard_map/reduce_scatter | solution.py:76
  581.2 2.0 convolution_bitcast_fusion
  583.2 1.8 convolution_convert_fusion
  585.1 130.9 %reduce-scatter.7.cloned.1.call-done = f32[256,256]{1,0:T(8,128)} async-done(((f32[4096,256]{1,0:T(8,128)}), f32[256,256]{1,0:T(8,128)}) %reduce-scatter.7.cloned.1.call-update) | async-done | bytes 262160 | tf_op jit(solution)/shard_map/reduce_scatter | solution.py:76
  716.0 1.7 multiply_convert_fusion.4
  717.7 144.9 %all-reduce.2.cloned.1.call-done = f32[256,256]{0,1:T(8,128)} async-done(((f32[256,256]{0,1:T(8,128)}), f32[256,256]{0,1:T(8,128)}) %all-reduce.2.cloned.1.call-update) | async-done | bytes 262160 | tf_op jit(solution)/shard_map/psum | solution.py:91
  862.6 1.8 copy.16
  (38 shorter events, 0.8 us)
Async XLA Ops:
  7.2 0.9 copy-start
  7.2 50.8 %all-gather.5.cloned.1.call-start = ((), (), s32[]{:S(2)}) async-start(), calls=%async_computation.4 | async-start | bytes 2228224 | tf_op jit(solution)/shard_map/all_gather | solution.py:63
  9.8 95.1 %all-gather.9.cloned.1.call-start = ((), (), s32[]{:S(2)}) async-start(), calls=%async_computation.8 | async-start | bytes 2228224 | tf_op jit(solution)/shard_map/all_gather | solution.py:63
  11.6 207.2 %reduce-scatter.5.cloned.1.call-start = ((), (), s32[]{:S(2)}) async-start(), calls=%async_computation.5 | async-start | bytes 3538944 | tf_op jit(solution)/shard_map/reduce_scatter | solution.py:69
  12.3 46.1 %copy-start.4 = (s32[256]{0:T(256)S(1)}, s32[256]{0:T(256)}, u32[]{:S(2)}) copy-start(s32[256]{0:T(256)} %param.23) | copy-start | bytes 3076
  12.3 46.1 %copy-start.5 = (s32[256]{0:T(256)S(1)}, s32[256]{0:T(256)}, u32[]{:S(2)}) copy-start(s32[256]{0:T(256)} %param.22) | copy-start | bytes 3076
  73.8 1.6 copy-start.1
  75.5 269.1 %reduce-scatter.9.cloned.1.call-start = ((), (), s32[]{:S(2)}) async-start(), calls=%async_computation.9 | async-start | bytes 3538944 | tf_op jit(solution)/shard_map/reduce_scatter | solution.py:69
  105.3 17.2 %copy-start.6 = (s32[1,384]{1,0:T(1,128)S(1)}, s32[1,384]{1,0:T(1,128)}, u32[]{:S(2)}) copy-start(s32[1,384]{1,0:T(1,128)} %param.27) | copy-start | bytes 4612
  105.3 17.2 %copy-start.7 = (f32[1,384]{1,0:T(1,128)S(1)}, f32[1,384]{1,0:T(1,128)}, u32[]{:S(2)}) copy-start(f32[1,384]{1,0:T(1,128)} %param.26) | copy-start | bytes 4612
  120.8 1.6 copy-start.2
  122.4 247.5 %all-gather.11.cloned.1.call-start = ((), (), s32[]{:S(2)}) async-start(), calls=%async_computation.10 | async-start | bytes 1769472 | tf_op jit(solution)/shard_map/all_gather | solution.py:71
  346.6 49.5 %all-gather.7.cloned.1.call-start = ((), (), s32[]{:S(2)}) async-start(), calls=%async_computation.6 | async-start | bytes 1769472 | tf_op jit(solution)/shard_map/all_gather | solution.py:71
  347.1 234.1 %reduce-scatter.11.cloned.1.call-start = ((), (), s32[]{:S(2)}) async-start(), calls=%async_computation.11 | async-start | bytes 4456448 | tf_op jit(solution)/shard_map/reduce_scatter | solution.py:76
  388.9 327.0 %reduce-scatter.7.cloned.1.call-start = ((), (), s32[]{:S(2)}) async-start(), calls=%async_computation.7 | async-start | bytes 4456448 | tf_op jit(solution)/shard_map/reduce_scatter | solution.py:76
  415.1 168.1 %copy-start.3 = (bf16[256,256]{1,0:T(8,128)(2,1)S(1)}, bf16[256,256]{1,0:T(8,128)(2,1)}, u32[]{:S(2)}) copy-start(bf16[256,256]{1,0:T(8,128)(2,1)} %param.20) | copy-start | bytes 393220
  415.1 447.5 %all-reduce.2.cloned.1.call-start = ((), (), s32[]{:S(2)}) async-start(), calls=%async_computation.12 | async-start | bytes 524288 | tf_op jit(solution)/shard_map/psum | solution.py:91
Sparse Core Ops, SparseCore 0:
  10.7 47.2 all-gather.4
  60.7 44.1 all-gather.8
  107.4 111.3 reduce-scatter.4
  221.1 123.4 reduce-scatter.8
  346.7 23.2 all-gather.10
  371.5 24.5 all-gather.6
  399.4 181.7 reduce-scatter.10
  584.9 130.9 reduce-scatter.6
  721.3 141.2 all-reduce.1
where the time goes:
time: 875 us; the launch traced here: 871 us
  waiting for transfers between devices  757 us (87%)
  other arithmetic  42.2 us (5%)
  local copies, waits for them, and re-layouts  34.1 us (4%)
  matrix products  22.5 us (3%)
  between operations  14.6 us (2%)
    reduce_scatter x2, waiting for transfers between devices, sweep(): lax.psum_scatter(back.reshape(vertex_blocks * tile, width), 'ecol', scatt...  296 us
    reduce_scatter x2, waiting for transfers between devices, sweep(): lax.psum_scatter(partial_value, 'vrow', scatter_dimension=0, tiled=True)  222 us
    psum x1, waiting for transfers between devices, shards(): grad_theta = lax.psum(local_theta, ('vrow', 'ecol'))  145 us
    all_gather x2, waiting for transfers between devices, sweep(): gathered = lax.all_gather(stacked, 'ecol', axis=0, tiled=True)  63.1 us
    scatter-add x4, other arithmetic, turn(): return total.at[target].add(masked)  32.6 us
    all_gather x2, waiting for transfers between devices, sweep(): column = lax.all_gather(scaled, 'vrow', axis=0, tiled=True)  29.8 us
  transfers between devices with their start and end apart: 9, of which 9 were waited for; matrix products, arithmetic and copies ran while one was open for 10% of the time, Pallas kernels for 0%

commit v1 on v0

v1 whole, which is shorter than its diff:
```python
import jax
import jax.numpy as jnp
from jax import lax
from jax.experimental import pallas as pl
from jax.experimental.pallas import tpu as pltpu
from jax.sharding import PartitionSpec as P

BF = jnp.bfloat16
F32 = jnp.float32
MESH = pl.DeviceIdType.MESH
T = 128
F = 256
VB = 32
EB = 24
SLOTS = 256
GF = (SLOTS + EB) // 2
GB = (SLOTS + VB) // 2
PARTS = 4
NSEM = 200


def plan(key, other, live, blocks, groups):
    t = jnp.arange(SLOTS, dtype=jnp.int32)
    alive = t < live
    key = jnp.where(alive, key, blocks)
    b = jnp.arange(blocks, dtype=jnp.int32)
    hit = key[:, None] == b[None, :]
    count = jnp.sum(hit.astype(jnp.int32), axis=0)
    padded = count + (count & 1)
    end = jnp.sum(jnp.where(b[None, :] <= b[:, None], padded[None, :], 0), axis=1)
    start = end - padded
    same = (key[:, None] == key[None, :]) & (t[None, :] < t[:, None])
    rank = jnp.sum(same.astype(jnp.int32), axis=1)
    place = jnp.sum(jnp.where(hit, start[None, :], 0), axis=1) + rank
    place = jnp.where(alive, place, -1)
    s = jnp.arange(2 * groups, dtype=jnp.int32)
    at = place[None, :] == s[:, None]
    tile = SLOTS + jnp.sum(jnp.where(at, t[None, :] - SLOTS, 0), axis=1)
    panel = jnp.sum(jnp.where(at, other[None, :], 0), axis=1)
    g2 = 2 * jnp.arange(groups, dtype=jnp.int32)
    keep = jnp.sum(
        ((start[None, :] < g2[:, None]) & (g2[:, None] < end[None, :])).astype(F32), axis=1
    )
    last = jnp.where(count > 0, end // 2, 0)
    return tile, panel, keep, last


def body(
    tile_f, panel_f, keep_f, last_f, tile_b, panel_b, keep_b, last_b,
    x_ref, g_ref, theta_ref, values_ref, vdeg_ref, ew_ref, ed_ref,
    y_ref, gx_ref, gt_ref, gw_ref,
    tiles, run, scale, theta_t,
    pt_z, pt_g, e_z, e_g,
    sib_s, sib_r, mine, zs, zr1, zr2, bxt, bzt, egt,
    vs, vr1, vr2, vkeep, ws, wr1, wr2, wkeep,
    gl, g1, gp1, g2, g3, go,
    tsem, ssem, rsem,
):
    i = lax.axis_index("vrow")
    j = lax.axis_index("ecol")
    z, core = i // 2, i % 2
    x, y = j // 4, j % 4

    def zc(d, c=None):
        return (((z + d) % 4) * 2 + (core if c is None else c), j)

    def xy(dx, dy):
        return (i, ((x + dx) % 4) * 4 + (y + dy) % 4)

    sib = (z * 2 + 1 - core, j)

    barrier = pltpu.get_barrier_semaphore()
    peers = [((i + d) % 8, j) for d in range(1, 8)]
    peers += [xy(d, 0) for d in (1, 2, 3)] + [xy(0, d) for d in (1, 2, 3)]
    for p in peers:
        pl.semaphore_signal(barrier, inc=1, device_id=p, device_id_type=MESH)

    load = pltpu.make_async_copy(values_ref, tiles.at[pl.ds(0, SLOTS)], tsem)
    load.start()

    deg = vdeg_ref[...].astype(F32)
    scale[...] = jnp.transpose(jnp.broadcast_to(1.0 / jnp.sqrt(deg), (F, 2 * T)))

    def prepare(src, dst):
        part = jnp.transpose(src[...].astype(F32) * scale[...]).astype(BF)
        for h in range(2):
            dst[2 * j + h] = part[:, h * T : (h + 1) * T]

    prepare(x_ref, pt_z)
    pl.semaphore_wait(barrier, len(peers))

    sent = []
    ids = [0]

    def send(src, dst, to):
        n = ids[0]
        ids[0] += 1
        copy = pltpu.make_async_remote_copy(
            src_ref=src, dst_ref=dst, send_sem=ssem.at[n], recv_sem=rsem.at[n],
            device_id=to, device_id_type=MESH,
        )
        copy.start()
        sent.append(copy)
        return copy

    def gather_row(pt):
        def block(h, a, b):
            dx, dy = (b, a) if h == 0 else (a, b)
            return pt.at[2 * (((x + dx) % 4) * 4 + (y + dy) % 4) + h]

        def to(h, a, b):
            return xy(b, a) if h == 0 else xy(a, b)

        def part(ref, up):
            return ref.at[pl.ds(0 if up else T, T)]

        def across(h, a):
            r = block(h, a, 0)
            return send(r, r, to(h, 0, 1)), send(r, r, to(h, 0, -1))

        def onward(h, a, b, up, where):
            r = part(block(h, a, b), up)
            return send(r, r, where)

        first, second, fwd = {}, {}, []
        for h in range(2):
            r = block(h, 0, 0)
            first[h] = send(r, r, to(h, 1, 0)), send(r, r, to(h, -1, 0))
        for h in range(2):
            second[h, 0] = across(h, 0)
        yield
        hop = {}
        for h in range(2):
            first[h][0].wait_recv()
            c = onward(h, -1, 0, True, to(h, 1, 0))
            first[h][1].wait_recv()
            hop[h] = c, onward(h, 1, 0, False, to(h, -1, 0))
        for h in range(2):
            second[h, -1] = across(h, -1)
            second[h, 1] = across(h, 1)
        yield

        def finish(a):
            for h in range(2):
                second[h, a][0].wait_recv()
                fwd.append(onward(h, a, -1, True, to(h, 0, 1)))
                second[h, a][1].wait_recv()
                fwd.append(onward(h, a, 1, False, to(h, 0, -1)))

        for h in range(2):
            for c in hop[h]:
                c.wait_recv()
            second[h, 2] = across(h, 2)
        finish(0)
        yield
        finish(-1)
        finish(1)
        yield
        finish(2)
        yield
        for c in fwd:
            c.wait_recv()

    def forward(pt, q):
        per = GF // PARTS
        unit = 5

        def turn(n, _):
            for u in range(unit):
                g = q * per + n * unit + u
                lhs = jnp.concatenate([pt[panel_f[2 * g]], pt[panel_f[2 * g + 1]]], axis=1)
                rhs = jnp.concatenate([tiles[tile_f[2 * g]], tiles[tile_f[2 * g + 1]]], axis=0)
                out = jnp.dot(lhs, rhs, preferred_element_type=F32)
                for h in range(2):
                    run[g + 1, h] = out[h * T : (h + 1) * T] + keep_f[g] * run[g, h]
            return 0

        lax.fori_loop(0, per // unit, turn, 0)

    def backward(e, q):
        per = GB // PARTS
        unit = 4

        def turn(n, _):
            for u in range(unit):
                g = q * per + n * unit + u
                lhs = jnp.concatenate([tiles[tile_b[2 * g]], tiles[tile_b[2 * g + 1]]], axis=1)
                rhs = jnp.concatenate([e[panel_b[2 * g]], e[panel_b[2 * g + 1]]], axis=0)
                out = jnp.dot(lhs, rhs, preferred_element_type=F32)
                for h in range(2):
                    run[g + 1, h] = out[:, h * T : (h + 1) * T] + keep_b[g] * run[g, h]
            return 0

        lax.fori_loop(0, per // unit, turn, 0)

    def reduce_col(k, finish):
        pair = {}
        for d in (2, 1, 3, 0):
            zd = (z + d) % 4
            for b in range(3):
                theirs = last_f[3 * (2 * zd + 1 - core) + b]
                ours = last_f[3 * (2 * zd + core) + b]
                for h in range(2):
                    rows = pl.ds(h * T, T)
                    sib_s[k, d, b, rows] = run[theirs, h].astype(BF)
                    mine[k, d, b, rows] = run[ours, h]
            pair[d] = send(sib_s.at[k, d], sib_r.at[k, d], sib)
        yield
        up, down = pl.ds(0, T), pl.ds(T, T)

        def join(d):
            pair[d].wait_recv()
            for b in range(3):
                mine[k, d, b] = mine[k, d, b] + sib_r[k, d, b].astype(F32)

        def pack(d, rows):
            for b in range(3):
                zs[k, d, b, rows] = mine[k, d, b, rows].astype(BF)

        join(2)
        pack(2, pl.ds(0, 2 * T))
        one = send(zs.at[k, 2, :, up], zr1.at[k, 0], zc(1))
        two = send(zs.at[k, 2, :, down], zr1.at[k, 1], zc(-1))
        join(1)
        pack(1, down)
        got = [send(zs.at[k, 1, :, down], zr2.at[k, 0, :, down], zc(1))]
        join(3)
        pack(3, up)
        got += [send(zs.at[k, 3, :, up], zr2.at[k, 1, :, up], zc(-1))]
        join(0)
        yield
        one.wait_recv()
        for b in range(3):
            zs[k, 1, b, up] = (mine[k, 1, b, up] + zr1[k, 0, b].astype(F32)).astype(BF)
        got += [send(zs.at[k, 1, :, up], zr2.at[k, 0, :, up], zc(1))]
        two.wait_recv()
        for b in range(3):
            zs[k, 3, b, down] = (mine[k, 3, b, down] + zr1[k, 1, b].astype(F32)).astype(BF)
        got += [send(zs.at[k, 3, :, down], zr2.at[k, 1, :, down], zc(-1))]
        yield
        for c in got:
            c.wait_recv()
        for b in range(3):
            total = mine[k, 0, b] + zr2[k, 0, b].astype(F32) + zr2[k, 1, b].astype(F32)
            finish(b, total)

    def split(value):
        hi = value.astype(BF)
        return hi, (value - hi.astype(F32)).astype(BF)

    def dot(a, b):
        return jnp.dot(a, b, preferred_element_type=F32)

    def coefs(b):
        cols = slice(b * T, (b + 1) * T)
        d = ed_ref[:, cols].astype(F32)
        return ew_ref[:, cols] / d, d

    def edges_z(b, total):
        hi, lo = split(total)
        bxt[b] = total
        bz = dot(theta_t[...], hi) + dot(theta_t[...], lo)
        bzt[b] = bz
        e_z[3 * i + b] = jnp.transpose(bz * coefs(b)[0]).astype(BF)

    def edges_g(b, total):
        coef, d = coefs(b)
        gw_ref[:, b * T : (b + 1) * T] = jnp.sum(bzt[b] * total, axis=0, keepdims=True) / d
        eg = total * coef
        egt[b] = eg
        hi, lo = split(eg)
        e_g[3 * i + b] = jnp.transpose(dot(theta_ref[...], hi) + dot(theta_ref[...], lo)).astype(BF)

    def gather_col(e):
        def shard(d, c=core):
            return e.at[pl.ds(3 * (2 * ((z + d) % 4) + c), 3)]

        def half(ref, up):
            return ref.at[:, pl.ds(0 if up else T // 2, T // 2)]

        def pass_on(ref, to):
            return send(ref, ref, to)

        right = pass_on(shard(0), zc(1))
        left = pass_on(shard(0), zc(-1))
        across = [pass_on(shard(0), sib)]
        yield
        right.wait_recv()
        far = [pass_on(half(shard(-1), True), zc(1))]
        left.wait_recv()
        far += [pass_on(half(shard(1), False), zc(-1))]
        across += [pass_on(shard(-1), sib), pass_on(shard(1), sib)]
        yield
        for c, up in zip(far, (True, False)):
            c.wait_recv()
            across += [pass_on(half(shard(2), up), sib)]
        yield
        for c in across:
            c.wait_recv()

    def reduce_row(k, out_ref):
        up, down = pl.ds(0, T // 2), pl.ds(T // 2, T // 2)

        def to(h, a, b):
            return xy(a, b) if h == 0 else xy(b, a)

        def fetch(h, p, q):
            dx, dy = (p, q) if h == 0 else (q, p)
            r = last_b[2 * (((x + dx) % 4) * 4 + (y + dy) % 4) + h]
            return jnp.concatenate([run[r, 0], run[r, 1]], axis=1)

        one, two, got = {}, {}, {}
        for h in range(2):
            for q in range(4):
                vs[k, h, 0, q] = fetch(h, 2, q).astype(BF)
            one[h] = send(vs.at[k, h, 0, :, up], vr1.at[k, h, 0], to(h, 1, 0))
            two[h] = send(vs.at[k, h, 0, :, down], vr1.at[k, h, 1], to(h, -1, 0))
        for h in range(2):
            for q in range(4):
                v = fetch(h, 1, q)
                vs[k, h, 1, q, down] = v[T // 2 :].astype(BF)
                vkeep[k, h, 1, q, up] = v[: T // 2]
                v = fetch(h, 3, q)
                vs[k, h, 2, q, up] = v[: T // 2].astype(BF)
                vkeep[k, h, 1, q, down] = v[T // 2 :]
            got[h] = [
                send(vs.at[k, h, 1, :, down], vr2.at[k, h, 0, :, down], to(h, 1, 0)),
                send(vs.at[k, h, 2, :, up], vr2.at[k, h, 1, :, up], to(h, -1, 0)),
            ]
        for h in range(2):
            for q in range(4):
                vkeep[k, h, 0, q] = fetch(h, 0, q)
        yield
        for h in range(2):
            one[h].wait_recv()
            for q in range(4):
                vs[k, h, 1, q, up] = (
                    vkeep[k, h, 1, q, up] + vr1[k, h, 0, q].astype(F32)
                ).astype(BF)
            got[h] += [send(vs.at[k, h, 1, :, up], vr2.at[k, h, 0, :, up], to(h, 1, 0))]
            two[h].wait_recv()
            for q in range(4):
                vs[k, h, 2, q, down] = (
                    vkeep[k, h, 1, q, down] + vr1[k, h, 1, q].astype(F32)
                ).astype(BF)
            got[h] += [send(vs.at[k, h, 2, :, down], vr2.at[k, h, 1, :, down], to(h, -1, 0))]
        yield
        one2, two2, got2 = {}, {}, {}
        for h in range(2):
            for c in got[h]:
                c.wait_recv()

            def total(q):
                return (
                    vkeep[k, h, 0, q]
                    + vr2[k, h, 0, q].astype(F32)
                    + vr2[k, h, 1, q].astype(F32)
                )

            ws[k, h, 0] = total(2).astype(BF)
            one2[h] = send(ws.at[k, h, 0, up], wr1.at[k, h, 0], to(h, 0, 1))
            two2[h] = send(ws.at[k, h, 0, down], wr1.at[k, h, 1], to(h, 0, -1))
            v = total(1)
            ws[k, h, 1, down] = v[T // 2 :].astype(BF)
            wkeep[k, h, 1, up] = v[: T // 2]
            v = total(3)
            ws[k, h, 2, up] = v[: T // 2].astype(BF)
            wkeep[k, h, 1, down] = v[T // 2 :]
            got2[h] = [
                send(ws.at[k, h, 1, down], wr2.at[k, h, 0, down], to(h, 0, 1)),
                send(ws.at[k, h, 2, up], wr2.at[k, h, 1, up], to(h, 0, -1)),
            ]
            wkeep[k, h, 0] = total(0)
        yield
        for h in range(2):
            one2[h].wait_recv()
            ws[k, h, 1, up] = (wkeep[k, h, 1, up] + wr1[k, h, 0].astype(F32)).astype(BF)
            got2[h] += [send(ws.at[k, h, 1, up], wr2.at[k, h, 0, up], to(h, 0, 1))]
            two2[h].wait_recv()
            ws[k, h, 2, down] = (wkeep[k, h, 1, down] + wr1[k, h, 1].astype(F32)).astype(BF)
            got2[h] += [send(ws.at[k, h, 2, down], wr2.at[k, h, 1, down], to(h, 0, -1))]
        yield
        for h in range(2):
            for c in got2[h]:
                c.wait_recv()
            v = wkeep[k, h, 0] + wr2[k, h, 0].astype(F32) + wr2[k, h, 1].astype(F32)
            rows = pl.ds(h * T, T)
            out_ref[rows] = (v * scale[rows]).astype(BF)

    def sum_theta():
        acc = jnp.zeros((F, F), F32)
        nt = (((1,), (1,)), ((), ()))
        for b in range(3):
            xh, xl = split(bxt[b])
            eh, el = split(egt[b])
            for a, c in ((xh, eh), (xl, eh), (xh, el)):
                acc = acc + lax.dot_general(a, c, nt, preferred_element_type=F32)
        gl[...] = acc
        got = []
        for d in range(1, 8):
            to = (i + d) % 8
            got.append(send(gl.at[pl.ds(32 * to, 32)], g1.at[d], (to, j)))
        yield
        own = gl[pl.ds(32 * i, 32)]
        for d, c in enumerate(got):
            c.wait_recv()
            own = own + g1[d + 1]
        gp1[...] = own
        got = []
        for d in (1, 2, 3):
            got.append(send(gp1.at[pl.ds(8 * ((x + d) % 4), 8)], g2.at[d], xy(d, 0)))
        yield
        own = gp1[pl.ds(8 * x, 8)]
        for d, c in enumerate(got):
            c.wait_recv()
            own = own + g2[d + 1]
        g3[y] = own
        got = [send(g3.at[y], g3.at[y], xy(0, d)) for d in (1, 2, 3)]
        yield
        for c in got:
            c.wait_recv()
        rows = pl.ds(32 * i + 8 * x, 8)
        go[rows] = ((g3[0] + g3[1]) + g3[2]) + g3[3]
        got = [send(go.at[rows], go.at[rows], xy(d, 0)) for d in (1, 2, 3)]
        yield
        for c in got:
            c.wait_recv()
        rows = pl.ds(32 * i, 32)
        got = [send(go.at[rows], go.at[rows], ((i + d) % 8, j)) for d in range(1, 8)]
        yield
        for c in got:
            c.wait_recv()
        gt_ref[...] = go[...]

    def step(gen):
        next(gen, None)

    def drain(gen):
        for _ in gen:
            pass

    row_z, row_g = gather_row(pt_z), gather_row(pt_g)
    step(row_z)
    prepare(g_ref, pt_g)
    theta_t[...] = jnp.transpose(theta_ref[...].astype(F32)).astype(BF)
    tiles[SLOTS] = jnp.zeros((T, T), BF)
    run[0] = jnp.zeros((2, T, T), F32)
    for _ in range(4):
        step(row_z)
    step(row_g)
    drain(row_z)
    load.wait()

    for q in range(PARTS):
        forward(pt_z, q)
        step(row_g)
    col_z, col_g = reduce_col(0, edges_z), reduce_col(1, edges_g)
    step(col_z)
    step(col_z)
    drain(row_g)
    forward(pt_g, 0)
    step(col_z)
    forward(pt_g, 1)
    drain(col_z)
    all_z, all_g = gather_col(e_z), gather_col(e_g)
    step(all_z)
    forward(pt_g, 2)
    step(all_z)
    forward(pt_g, 3)
    step(col_g)
    step(all_z)
    step(col_g)
    drain(all_z)
    backward(e_z, 0)
    step(col_g)
    backward(e_z, 1)
    drain(col_g)
    step(all_g)
    theta = sum_theta()
    step(theta)
    backward(e_z, 2)
    step(all_g)
    backward(e_z, 3)
    back_z, back_g = reduce_row(0, y_ref), reduce_row(1, gx_ref)
    step(back_z)
    step(all_g)
    step(theta)
    drain(all_g)
    backward(e_g, 0)
    step(back_z)
    step(theta)
    backward(e_g, 1)
    step(theta)
    step(back_z)
    backward(e_g, 2)
    step(theta)
    step(back_z)
    backward(e_g, 3)
    step(back_g)
    drain(back_z)
    drain(back_g)
    drain(theta)
    for c in sent:
        c.wait_send()


def shards(
    features, grad_out, theta, tile_values, tile_rows, tile_cols, tile_count,
    vertex_degree, edge_weight, edge_degree,
):
    live = tile_count[0]
    by_col = plan(tile_cols, tile_rows, live, EB, GF)
    by_row = plan(tile_rows, tile_cols, live, VB, GB)
    smem = pl.BlockSpec(memory_space=pltpu.SMEM)
    vmem = pl.BlockSpec(memory_space=pltpu.VMEM)
    hbm = pl.BlockSpec(memory_space=pl.ANY)
    v = pltpu.VMEM
    scratch = [
        v((SLOTS + 1, T, T), BF),
        v((GB + 1, 2, T, T), F32),
        v((2 * T, F), F32),
        v((F, F), BF),
        v((VB, F, T), BF),
        v((VB, F, T), BF),
        v((EB, T, F), BF),
        v((EB, T, F), BF),
        v((2, 4, 3, F, T), BF),
        v((2, 4, 3, F, T), BF),
        v((2, 4, 3, F, T), F32),
        v((2, 4, 3, F, T), BF),
        v((2, 2, 3, T, T), BF),
        v((2, 2, 3, F, T), BF),
        v((3, F, T), F32),
        v((3, F, T), F32),
        v((3, F, T), F32),
        v((2, 2, 3, 4, T, F), BF),
        v((2, 2, 2, 4, T // 2, F), BF),
        v((2, 2, 2, 4, T, F), BF),
        v((2, 2, 2, 4, T, F), F32),
        v((2, 2, 3, T, F), BF),
        v((2, 2, 2, T // 2, F), BF),
        v((2, 2, 2, T, F), BF),
        v((2, 2, 2, T, F), F32),
        v((F, F), F32),
        v((8, 32, F), F32),
        v((32, F), F32),
        v((4, 8, F), F32),
        v((4, 8, F), F32),
        v((F, F), F32),
        pltpu.SemaphoreType.DMA,
        pltpu.SemaphoreType.DMA((NSEM,)),
        pltpu.SemaphoreType.DMA((NSEM,)),
    ]
    return pl.pallas_call(
        body,
        out_shape=(
            jax.ShapeDtypeStruct((2 * T, F), BF),
            jax.ShapeDtypeStruct((2 * T, F), BF),
            jax.ShapeDtypeStruct((F, F), F32),
            jax.ShapeDtypeStruct((1, 3 * T), F32),
        ),
        in_specs=[smem] * 8 + [vmem] * 3 + [hbm] + [vmem] * 3,
        out_specs=[vmem] * 4,
        scratch_shapes=scratch,
        compiler_params=pltpu.CompilerParams(
            collective_id=0, has_side_effects=True, vmem_limit_bytes=62 * 1024 * 1024
        ),
        cost_estimate=pl.CostEstimate(
            flops=20_000_000_000, bytes_accessed=10_000_000, transcendentals=0
        ),
    )(
        *by_col, *by_row, features, grad_out, theta, tile_values,
        vertex_degree.reshape(1, 2 * T), edge_weight, edge_degree,
    )


def solution(mesh):
    both = ("vrow", "ecol")
    in_specs = (
        P(both, None), P(both, None), P(), P(both, None, None), P(both), P(both), P(both),
        P(both), P("ecol", "vrow"), P("ecol", "vrow"),
    )
    out_specs = (P(both, None), P(both, None), P(), P("ecol", "vrow"))
    return jax.shard_map(shards, mesh=mesh, in_specs=in_specs, out_specs=out_specs, check_vma=False)
```

time: 875 us -> 130 us (0.15)
  waiting for transfers between devices: 757 us -> 0 us
  Pallas kernels: 0 us -> 114 us
  other arithmetic: 42.2 us -> 8.86 us
  local copies, waits for them, and re-layouts: 34.1 us -> 6.04 us
  matrix products: 22.5 us -> 0 us
  between operations: 14.6 us -> 1.31 us
    reduce_scatter x4 -> x0, waiting for transfers between devices: 518 us -> none  [the longest x2 296 us: sweep(): lax.psum_scatter(back.reshape(vertex_blocks * tile, width), 'ecol', scatt...]
    psum x1 -> x0, waiting for transfers between devices: 145 us -> none  [shards(): grad_theta = lax.psum(local_theta, ('vrow', 'ecol'))]
    pallas_call x0 -> x1, Pallas kernels: none -> 114 us  [shards(): pl.pallas_call(body, out_shape=(jax.ShapeDtypeStruct((2 * T, F), BF), jax...]
    all_gather x4 -> x0, waiting for transfers between devices: 93 us -> none  [the longest x2 63.1 us: sweep(): gathered = lax.all_gather(stacked, 'ecol', axis=0, tiled=True)]
    scatter-add x4 -> x0, other arithmetic: 32.6 us -> none  [turn(): return total.at[target].add(masked)]
    dot_general x7 -> x0, matrix products: 22.5 us -> none  [the longest x2 9.17 us: turn(): jnp.einsum('tvc,tvw->tcw', vals, picked, preferred_element_type=jnp.float32)]
    while x1 -> x0, local copies, waits for them, and re-layouts: 12 us -> none  [accumulate(): return lax.fori_loop(0, blocks, turn, init)]
    gather x4 -> x0, local copies, waits for them, and re-layouts: 11.3 us -> none  [the longest x2 7.16 us: turn(): picked = panels[rws]]
  transfers between devices with their start and end apart: 9 -> 0, of which waited for: 9 -> 0; matrix products, arithmetic and copies ran while one was open for 10% -> 0% of each run, Pallas kernels for 0% -> 0%
where the time goes in v1:
time: 130 us
  Pallas kernels  114 us (88%)
  other arithmetic  8.86 us (7%)
  local copies, waits for them, and re-layouts  6.04 us (5%)
  between operations  1.31 us (1%)
    pallas_call x1, Pallas kernels, shards(): pl.pallas_call(body, out_shape=(jax.ShapeDtypeStruct((2 * T, F), BF), jax...  114 us
    unnamed x4, local copies, waits for them, and re-layouts  6.04 us
    reduce_sum x2, other arithmetic, plan(): panel = jnp.sum(jnp.where(at, other[None, :], 0), axis=1)  2.88 us

profile of v1, /device:TPU:0, one launch (start us, length us, event | category | flops | bytes accessed | tf_op | source)
XLA Modules:
  0.0 129.7 jit_solution(4038864834580498967)
XLA Ops:
  1.3 0.7 fusion.2
  2.0 0.1 convert_reduce_fusion.3
  2.1 0.1 select_reduce_fusion.6
  2.2 0.6 compare_select_fusion
  2.8 0.7 fusion.3
  3.4 0.1 convert_reduce_fusion.5
  3.6 0.1 select_reduce_fusion.7
  3.7 0.5 compare_select_fusion.1
  4.2 0.1 select_reduce_fusion.5
  4.3 0.2 convert_reduce_fusion.1
  4.5 0.1 select_reduce_fusion.4
  4.6 0.2 convert_reduce_fusion
  4.8 0.7 convert_reduce_fusion.4.keep_f
  5.4 0.7 convert_reduce_fusion.2.keep_b
  6.1 1.4 %select_reduce_fusion = (s32[288]{0:T(512)}, s32[288]{0:T(512)S(1)}) fusion(s32[256]{0:T(256)} %param.15, s32[256]{0:T(256)S(1)} %get-tuple-element.12, s32[256]{0:T(256)S(1)} %iota_add_fusion), kind=kLoop, calls=%fused_computation | loop fusion | flops 368064 | bytes 5376 | tf_op jit(solution)/shard_map/reduce_sum | solution.py:39
  7.6 0.6 broadcast_add_fusion.tile_b
  8.1 1.4 %select_reduce_fusion.2 = (s32[280]{0:T(512)}, s32[280]{0:T(512)S(1)}) fusion(s32[256]{0:T(256)} %param.14, s32[256]{0:T(256)S(1)} %get-tuple-element.13, s32[256]{0:T(256)S(1)} %iota_add_fusion), kind=kLoop, calls=%fused_computation.3 | loop fusion | flops 357840 | bytes 5312 | tf_op jit(solution)/shard_map/reduce_sum | solution.py:39
  9.6 0.6 broadcast_add_fusion.1.tile_f
  10.2 113.5 %shard_map.129 = (bf16[256,256]{1,0:T(8,128)(2,1)}, bf16[256,256]{1,0:T(8,128)(2,1)}, f32[256,256]{1,0:T(8,128)}, f32[1,384]{1,0:T(1,128)}) custom-call(s32[280]{0:T(512)} %broadcast_add_fusion.1.tile_f, s32[280]{0:T(512)} %get-tuple-element.6.panel_f, f32[140]{0:T(256)} %convert_reduce_fusion.4.keep_f, s32[24]{0:T(128)} %get-tuple-element.10.last_f, ...), custom_call_target="tpu_custom_call" | custom-call | flops 20000000000 | bytes 10000000 | tf_op jit(solution)/shard_map/pallas_call | solution.py:554
  123.7 1.6 %copy.19 = bf16[256,256]{1,0:T(8,128)(2,1)} copy(bf16[256,256]{1,0:T(8,128)(2,1)} %get-tuple-element.18) | data formatting | bytes 262144
  125.3 1.6 %copy.20 = bf16[256,256]{1,0:T(8,128)(2,1)} copy(bf16[256,256]{1,0:T(8,128)(2,1)} %get-tuple-element.19) | data formatting | bytes 262144
  126.8 1.7 %copy.21 = f32[256,256]{1,0:T(8,128)} copy(f32[256,256]{1,0:T(8,128)} %get-tuple-element.20) | data formatting | bytes 524288
  128.5 1.2 copy.22
  (6 shorter events, 0.0 us)

commit v2 on v0

v2 whole, which is shorter than its diff:
```python
import jax
import jax.numpy as jnp
from jax import lax
from jax.experimental import pallas as pl
from jax.experimental.pallas import tpu as pltpu
from jax.sharding import PartitionSpec as P

BF = jnp.bfloat16
F32 = jnp.float32
MESH = pl.DeviceIdType.MESH
T = 128
F = 256
VB = 32
EB = 24
SLOTS = 256
GF = (SLOTS + EB) // 2
GB = (SLOTS + VB) // 2
PARTS = 2
NSEND = 29
NRECV = 57


def plan(key, other, live, pad):
    n = SLOTS

    def iota(shape, dim):
        return lax.broadcasted_iota(jnp.int32, shape, dim).astype(F32)

    key_l = jnp.broadcast_to(key.astype(F32), (n, n))
    key_l = jnp.where(iota((n, n), 1) < live, key_l, float(n))
    key_s = jnp.transpose(key_l)
    other_s = jnp.transpose(jnp.broadcast_to(other.astype(F32), (n, n)))
    t = iota((n, n), 0)
    same = jnp.where((key_s == key_l) & (iota((n, n), 1) < t), 1.0, 0.0)
    rank = jnp.sum(same, axis=1, keepdims=True)
    hit = jnp.where(key_s[:, :T] == iota((n, T), 1), 1.0, 0.0)
    count = jnp.sum(hit, axis=0, keepdims=True)
    half = jnp.floor((count + 1.0) * 0.5)
    upto = jnp.where(iota((T, T), 0) <= iota((T, T), 1), 1.0, 0.0)
    end = jnp.dot(
        jnp.broadcast_to(half, (8, T)).astype(BF), upto.astype(BF), preferred_element_type=F32
    )[:1]
    start = 2.0 * (end - half)
    place = jnp.sum(hit * start, axis=1, keepdims=True) + rank
    place = jnp.where(key_s[:, :1] < float(n), place, -1.0)
    at = jnp.where(place == iota((n, pad), 1), 1.0, 0.0)
    tile = jnp.sum(at * (t[:, :1] - float(n)), axis=0, keepdims=True) + float(n)
    panel = jnp.sum(at * other_s[:, :1], axis=0, keepdims=True)
    more = jnp.where(rank > 0.0, 1.0, 0.0)
    keep = jnp.sum(jnp.where(place == 2.0 * iota((n, pad), 1), more, 0.0), axis=0, keepdims=True)
    last = jnp.where(count > 0.0, end, 0.0)
    last = jnp.concatenate([last, jnp.zeros((1, pad - T), F32)], axis=1)
    rows = jnp.concatenate([tile, panel, keep, last, jnp.zeros((4, pad), F32)], axis=0)
    return rows.astype(jnp.int32)


def order_tiles(count_ref, rows_ref, cols_ref, by_col, by_row):
    live = count_ref[0].astype(F32)
    by_col[...] = plan(cols_ref[...], rows_ref[...], live, 384)
    by_row[...] = plan(rows_ref[...], cols_ref[...], live, 384)


def body(
    by_col, by_row,
    x_ref, g_ref, theta_ref, values_ref, vdeg_ref, ew_ref, ed_ref,
    y_ref, gz_ref, gt_ref, gw_ref,
    tiles, run, scale, theta_t,
    pt_0, pt_1, pt_2, pt_3, e_0, e_1, e_2, e_3,
    sib_s, sib_r, mine, zs, zr, bxt, bgt, vs, vr, vkeep, ws, wr,
    gl, g1, gp1, g2, g3, go,
    tsem, ssem, rsem,
):
    pts, es = (pt_0, pt_1, pt_2, pt_3), (e_0, e_1, e_2, e_3)
    i = lax.axis_index("vrow")
    j = lax.axis_index("ecol")
    z, core = i // 2, i % 2
    x, y = j // 4, j % 4

    def zc(d, c=None):
        return (((z + d) % 4) * 2 + (core if c is None else c), j)

    def xy(dx, dy):
        return (i, ((x + dx) % 4) * 4 + (y + dy) % 4)

    sib = (z * 2 + 1 - core, j)

    barrier = pltpu.get_barrier_semaphore()
    peers = [((i + d) % 8, j) for d in range(1, 8)]
    peers += [xy(d, 0) for d in (1, 2, 3)] + [xy(0, d) for d in (1, 2, 3)]
    for p in peers:
        pl.semaphore_signal(barrier, inc=1, device_id=p, device_id_type=MESH)

    load = pltpu.make_async_copy(values_ref, tiles.at[pl.ds(0, SLOTS)], tsem)
    load.start()

    deg = vdeg_ref[...].astype(F32)
    scale[...] = jnp.transpose(jnp.broadcast_to(1.0 / jnp.sqrt(deg), (F, 2 * T)))

    def prepare(src, k):
        part = jnp.transpose(src[...].astype(F32) * scale[...]).astype(BF)
        for c in range(2):
            for h in range(2):
                pts[k + c][2 * j + h] = part[c * T : (c + 1) * T, h * T : (h + 1) * T]

    prepare(x_ref, 0)
    pl.semaphore_wait(barrier, len(peers))

    sends, groups = [], [0, 0]

    def send(src, dst, to, out, into):
        pltpu.make_async_remote_copy(
            src_ref=src, dst_ref=dst, send_sem=ssem.at[out], recv_sem=rsem.at[into],
            device_id=to, device_id_type=MESH,
        ).start()

    def leaving(ref):
        n = groups[0]
        groups[0] += 1
        sends.append((ref, n))
        return n

    def coming():
        groups[1] += 1
        return groups[1] - 1

    def arrived(ref, n):
        pltpu.make_async_copy(ref, ref, rsem.at[n]).wait()

    near = (1, 3, 2)

    def gather_row(k):
        pt = pts[k]

        def to(h, a, b):
            return xy(b, a) if h == 0 else xy(a, b)

        out, one, two = leaving(pt.at[pl.ds(0, 30)]), coming(), coming()
        own = [pt.at[2 * j + h] for h in range(2)]
        for d in near:
            for h in range(2):
                send(own[h], own[h], to(h, d, 0), out, one)
        for d in near:
            for h in range(2):
                send(own[h], own[h], to(h, 0, d), out, two)
        yield
        arrived(pt.at[pl.ds(0, 6)], one)
        for a in near:
            for d in near:
                for h in range(2):
                    dx, dy = (0, a) if h == 0 else (a, 0)
                    r = pt.at[2 * (((x + dx) % 4) * 4 + (y + dy) % 4) + h]
                    send(r, r, to(h, 0, d), out, two)
        yield
        arrived(pt.at[pl.ds(0, 24)], two)

    def sweep(table, groups, unit, part, product):
        per = groups // PARTS

        def turn(n, acc):
            for u in range(unit):
                g = part * per + n * unit + u
                acc = product(2 * g) + table[2, g].astype(F32) * acc
                run[g + 1] = acc
            return acc

        lax.fori_loop(0, per // unit, turn, run[part * per])

    def dot(a, b):
        return jnp.dot(a, b, preferred_element_type=F32)

    def forward(k, part):
        pt = pts[k]

        def product(s):
            lhs = jnp.concatenate([pt[by_col[1, s]], pt[by_col[1, s + 1]]], axis=1)
            rhs = jnp.concatenate([tiles[by_col[0, s]], tiles[by_col[0, s + 1]]], axis=0)
            return dot(lhs, rhs)

        sweep(by_col, GF, 35, part, product)

    def backward(k, part):
        e = es[k]

        def product(s):
            lhs = jnp.concatenate([tiles[by_row[0, s]], tiles[by_row[0, s + 1]]], axis=1)
            rhs = jnp.concatenate([e[by_row[1, s]], e[by_row[1, s + 1]]], axis=0)
            return dot(lhs, rhs)

        sweep(by_row, GB, 36, part, product)

    def split(value):
        hi = value.astype(BF)
        return hi, (value - hi.astype(F32)).astype(BF)

    def coefs(b):
        cols = slice(b * T, (b + 1) * T)
        d = ed_ref[:, cols].astype(F32)
        return ew_ref[:, cols] / d, d

    def reduce_col(k):
        order = (2, 1, 3, 0)
        out, out2 = leaving(sib_s.at[k]), leaving(zs.at[k])
        pair, into = [coming() for _ in range(4)], coming()
        for d in order:
            zd = (z + d) % 4
            for b in range(3):
                sib_s[k, d, b] = run[by_col[3, 3 * (2 * zd + 1 - core) + b]].astype(BF)
            send(sib_s.at[k, d], sib_r.at[k, d], sib, out, pair[d])
        for d in order:
            zd = (z + d) % 4
            for b in range(3):
                mine[k, d, b] = run[by_col[3, 3 * (2 * zd + core) + b]]
        yield
        for d in order:
            arrived(sib_r.at[k, d], pair[d])
            for b in range(3):
                total = mine[k, d, b] + sib_r[k, d, b].astype(F32)
                if d == 0:
                    mine[k, 0, b] = total
                else:
                    zs[k, d - 1, b] = total.astype(BF)
            if d:
                send(zs.at[k, d - 1], zr.at[k, d - 1], zc(d), out2, into)
        yield
        arrived(zr.at[k], into)
        for b in range(3):
            total = mine[k, 0, b]
            for d in (1, 2, 3):
                total = total + zr[k, d - 1, b].astype(F32)
            if k < 2:
                bxt[k, b] = total
            else:
                bgt[k - 2, b] = total
            es[k][3 * i + b] = jnp.transpose(total * coefs(b)[0]).astype(BF)

    def gather_col(k):
        def shard(d):
            return es[k].at[pl.ds(3 * (2 * ((z + d) % 4) + core), 3)]

        out, across = leaving(es[k].at[pl.ds(0, 21)]), coming()
        own = {d: coming() for d in (2, 1, 3)}
        for d in own:
            send(shard(0), shard(0), zc(d), out, own[d])
        send(shard(0), shard(0), sib, out, across)

        def pass_on(d):
            arrived(shard(-d), own[d])
            send(shard(-d), shard(-d), sib, out, across)

        yield
        pass_on(1)
        pass_on(3)
        yield
        pass_on(2)
        yield
        arrived(es[k].at[pl.ds(0, 12)], across)

    def weights_grad():
        for b in range(3):
            hi, lo = zip(*[split(bxt[c, b]) for c in range(2)])
            hi, lo = jnp.concatenate(hi, axis=0), jnp.concatenate(lo, axis=0)
            bz = dot(theta_t[...], hi) + dot(theta_t[...], lo)
            terms = bz[:T] * bgt[0, b] + bz[T:] * bgt[1, b]
            cols = slice(b * T, (b + 1) * T)
            gw_ref[:, cols] = jnp.sum(terms, axis=0, keepdims=True) / coefs(b)[1]

    def reduce_row(k):
        def to(h, a, b):
            return xy(a, b) if h == 0 else xy(b, a)

        def fetch(h, p, q):
            dx, dy = (p, q) if h == 0 else (q, p)
            return run[by_row[3, 2 * (((x + dx) % 4) * 4 + (y + dy) % 4) + h]]

        out, out2, one, two = leaving(vs.at[k]), leaving(ws.at[k]), coming(), coming()
        for p in near:
            for h in range(2):
                for q in range(4):
                    vs[k, h, p - 1, q] = fetch(h, p, q).astype(BF)
                send(vs.at[k, h, p - 1], vr.at[k, h, p - 1], to(h, p, 0), out, one)
        for h in range(2):
            for q in range(4):
                vkeep[k, h, q] = fetch(h, 0, q)
        yield
        arrived(vr.at[k], one)
        for q in (1, 3, 2, 0):
            for h in range(2):
                total = vkeep[k, h, q]
                for p in range(3):
                    total = total + vr[k, h, p, q].astype(F32)
                if q:
                    ws[k, h, q - 1] = total.astype(BF)
                    send(ws.at[k, h, q - 1], wr.at[k, h, q - 1], to(h, 0, q), out2, two)
                else:
                    vkeep[k, h, 0] = total
        yield
        arrived(wr.at[k], two)
        for h in range(2):
            v = vkeep[k, h, 0]
            for q in range(3):
                v = v + wr[k, h, q].astype(F32)
            rows = pl.ds(h * T, T)
            cols = pl.ds((k % 2) * T, T)
            v = v * scale[rows, :T]
            if k < 2:
                y_ref[rows, cols] = v
            else:
                gz_ref[rows, cols] = v.astype(BF)

    def sum_theta():
        nt = (((1,), (1,)), ((), ()))
        for w in range(2):
            acc = jnp.zeros((F, T), F32)
            for b in range(3):
                xs = [split(bxt[c, b]) for c in range(2)]
                xh, xl = [jnp.concatenate([p[m] for p in xs], axis=0) for m in range(2)]
                eh, el = split(bgt[w, b] * coefs(b)[0])
                for p, q in ((xh, eh), (xl, eh), (xh, el)):
                    acc = acc + lax.dot_general(p, q, nt, preferred_element_type=F32)
            gl[:, w * T : (w + 1) * T] = acc
        out = [leaving(gl.at[pl.ds(0, 224)]), leaving(gp1.at[pl.ds(0, 24)]), leaving(g3.at[pl.ds(0, 3)])]
        out += [leaving(go.at[pl.ds(0, 24)]), leaving(go.at[pl.ds(0, 224)])]
        into = [coming() for _ in range(5)]
        for d in range(1, 8):
            to = (i + d) % 8
            send(gl.at[pl.ds(32 * to, 32)], g1.at[d - 1], (to, j), out[0], into[0])
        yield
        arrived(g1, into[0])
        own = gl[pl.ds(32 * i, 32)]
        for d in range(7):
            own = own + g1[d]
        gp1[...] = own
        for d in near:
            send(gp1.at[pl.ds(8 * ((x + d) % 4), 8)], g2.at[d - 1], xy(d, 0), out[1], into[1])
        yield
        arrived(g2, into[1])
        g3[y] = gp1[pl.ds(8 * x, 8)] + g2[0] + g2[1] + g2[2]
        for d in near:
            send(g3.at[y], g3.at[y], xy(0, d), out[2], into[2])
        yield
        arrived(g3.at[pl.ds(0, 3)], into[2])
        rows = pl.ds(32 * i + 8 * x, 8)
        go[rows] = ((g3[0] + g3[1]) + g3[2]) + g3[3]
        for d in near:
            send(go.at[rows], go.at[rows], xy(d, 0), out[3], into[3])
        yield
        arrived(go.at[pl.ds(0, 24)], into[3])
        rows = pl.ds(32 * i, 32)
        for d in range(1, 8):
            send(go.at[rows], go.at[rows], ((i + d) % 8, j), out[4], into[4])
        yield
        arrived(go.at[pl.ds(0, 224)], into[4])
        gt_ref[...] = go[...]

    def step(gen):
        next(gen, None)

    def drain(gen):
        for _ in gen:
            pass

    row = [gather_row(k) for k in range(4)]
    col = [reduce_col(k) for k in range(4)]
    full = [gather_col(k) for k in range(4)]
    back = [reduce_row(k) for k in range(4)]
    theta = sum_theta()
    def tables():
        theta_t[...] = jnp.transpose(theta_ref[...].astype(F32)).astype(BF)
        tiles[SLOTS] = jnp.zeros((T, T), BF)
        run[0] = jnp.zeros((T, T), F32)

    step(row[0])
    step(row[1])
    prepare(g_ref, 2)
    step(row[2])
    tables()
    step(row[3])
    step(row[0])
    step(row[1])
    step(row[2])
    step(row[3])
    step(row[0])
    load.wait()
    forward(0, 0)
    forward(0, 1)
    step(col[0])
    step(row[1])
    forward(1, 0)
    step(col[0])
    forward(1, 1)
    step(col[1])
    step(row[2])
    forward(2, 0)
    step(col[1])
    forward(2, 1)
    step(col[2])
    step(row[3])
    forward(3, 0)
    step(col[0])
    step(full[0])
    step(col[2])
    forward(3, 1)
    step(col[3])
    step(col[1])
    step(full[1])
    step(col[3])
    step(full[0])
    step(full[0])
    step(full[0])
    backward(0, 0)
    backward(0, 1)
    step(back[0])
    step(col[2])
    step(full[2])
    step(full[1])
    step(full[1])
    step(full[1])
    backward(1, 0)
    backward(1, 1)
    step(col[3])
    step(theta)
    step(back[0])
    step(back[1])
    weights_grad()
    step(full[3])
    step(full[2])
    step(full[2])
    step(full[2])
    backward(2, 0)
    step(back[0])
    backward(2, 1)
    step(theta)
    step(back[2])
    step(full[3])
    step(full[3])
    step(theta)
    step(back[1])
    step(full[3])
    backward(3, 0)
    backward(3, 1)
    step(back[3])
    step(theta)
    step(back[2])
    step(back[1])
    step(theta)
    step(back[3])
    step(back[2])
    step(back[3])
    step(theta)
    for ref, n in sends:
        pltpu.make_async_copy(ref, ref, ssem.at[n]).wait()


def tail(ys_ref, gz_ref, gt_ref, gw_ref, theta_ref, y_out, gx_out, gt_out, gw_out):
    theta = theta_ref[...]
    ys = ys_ref[...]
    hi = ys.astype(BF)
    lo = (ys - hi.astype(F32)).astype(BF)
    y = jnp.dot(hi, theta, preferred_element_type=F32)
    y_out[...] = (y + jnp.dot(lo, theta, preferred_element_type=F32)).astype(BF)
    nt = (((1,), (1,)), ((), ()))
    gx_out[...] = lax.dot_general(gz_ref[...], theta, nt, preferred_element_type=F32).astype(BF)
    gt_out[...] = gt_ref[...]
    gw_out[...] = gw_ref[...]


def shards(
    features, grad_out, theta, tile_values, tile_rows, tile_cols, tile_count,
    vertex_degree, edge_weight, edge_degree,
):
    smem = pl.BlockSpec(memory_space=pltpu.SMEM)
    vmem = pl.BlockSpec(memory_space=pltpu.VMEM)
    hbm = pl.BlockSpec(memory_space=pl.ANY)
    v = pltpu.VMEM
    scratch = [
        v((SLOTS + 1, T, T), BF),
        v((GB + 1, T, T), F32),
        v((2 * T, F), F32),
        v((F, F), BF),
        *[v((VB, T, T), BF)] * 4,
        *[v((EB, T, T), BF)] * 4,
        v((4, 4, 3, T, T), BF),
        v((4, 4, 3, T, T), BF),
        v((4, 4, 3, T, T), F32),
        v((4, 3, 3, T, T), BF),
        v((4, 3, 3, T, T), BF),
        v((2, 3, T, T), F32),
        v((2, 3, T, T), F32),
        v((4, 2, 3, 4, T, T), BF),
        v((4, 2, 3, 4, T, T), BF),
        v((4, 2, 4, T, T), F32),
        v((4, 2, 3, T, T), BF),
        v((4, 2, 3, T, T), BF),
        v((F, F), F32),
        v((7, 32, F), F32),
        v((32, F), F32),
        v((3, 8, F), F32),
        v((4, 8, F), F32),
        v((F, F), F32),
        pltpu.SemaphoreType.DMA,
        pltpu.SemaphoreType.DMA((NSEND,)),
        pltpu.SemaphoreType.DMA((NRECV,)),
    ]
    table = jax.ShapeDtypeStruct((8, 384), jnp.int32)
    by_col, by_row = pl.pallas_call(
        order_tiles,
        out_shape=(table, table),
        in_specs=[smem, vmem, vmem],
        out_specs=[vmem] * 2,
        cost_estimate=pl.CostEstimate(flops=1_000_000, bytes_accessed=30_000, transcendentals=0),
    )(tile_count, tile_rows.reshape(1, SLOTS), tile_cols.reshape(1, SLOTS))
    ys, gz, gt, gw = pl.pallas_call(
        body,
        out_shape=(
            jax.ShapeDtypeStruct((2 * T, F), F32),
            jax.ShapeDtypeStruct((2 * T, F), BF),
            jax.ShapeDtypeStruct((F, F), F32),
            jax.ShapeDtypeStruct((1, 3 * T), F32),
        ),
        in_specs=[smem] * 2 + [vmem] * 3 + [hbm] + [vmem] * 3,
        out_specs=[vmem] * 4,
        scratch_shapes=scratch,
        compiler_params=pltpu.CompilerParams(
            collective_id=0, has_side_effects=True, vmem_limit_bytes=60 * 1024 * 1024
        ),
        cost_estimate=pl.CostEstimate(
            flops=20_000_000_000, bytes_accessed=10_000_000, transcendentals=0
        ),
    )(
        by_col, by_row, features, grad_out, theta, tile_values, vertex_degree.reshape(1, 2 * T),
        edge_weight, edge_degree,
    )
    return pl.pallas_call(
        tail,
        out_shape=(
            jax.ShapeDtypeStruct((2 * T, F), BF),
            jax.ShapeDtypeStruct((2 * T, F), BF),
            jax.ShapeDtypeStruct((F, F), F32),
            jax.ShapeDtypeStruct((1, 3 * T), F32),
        ),
        in_specs=[vmem] * 5,
        out_specs=[vmem] * 4,
        cost_estimate=pl.CostEstimate(flops=100_000_000, bytes_accessed=2_000_000, transcendentals=0),
    )(ys, gz, gt, gw, theta)


def solution(mesh):
    both = ("vrow", "ecol")
    in_specs = (
        P(both, None), P(both, None), P(), P(both, None, None), P(both), P(both), P(both),
        P(both), P("ecol", "vrow"), P("ecol", "vrow"),
    )
    out_specs = (P(both, None), P(both, None), P(), P("ecol", "vrow"))
    return jax.shard_map(shards, mesh=mesh, in_specs=in_specs, out_specs=out_specs, check_vma=False)
```

time: 875 us -> 98.3 us (0.11)
  waiting for transfers between devices: 757 us -> 0 us
  Pallas kernels: 0 us -> 95.7 us
  other arithmetic: 42.2 us -> 0 us
  local copies, waits for them, and re-layouts: 34.1 us -> 0 us
  matrix products: 22.5 us -> 0 us
  between operations: 14.6 us -> 1.29 us
    reduce_scatter x4 -> x0, waiting for transfers between devices: 518 us -> none  [the longest x2 296 us: sweep(): lax.psum_scatter(back.reshape(vertex_blocks * tile, width), 'ecol', scatt...]
    psum x1 -> x0, waiting for transfers between devices: 145 us -> none  [shards(): grad_theta = lax.psum(local_theta, ('vrow', 'ecol'))]
    pallas_call x0 -> x3, Pallas kernels: none -> 95.7 us  [the longest x1 91.5 us: shards(): pl.pallas_call(body, out_shape=(jax.ShapeDtypeStruct((2 * T, F), F32), ja...]
    all_gather x4 -> x0, waiting for transfers between devices: 93 us -> none  [the longest x2 63.1 us: sweep(): gathered = lax.all_gather(stacked, 'ecol', axis=0, tiled=True)]
    scatter-add x4 -> x0, other arithmetic: 32.6 us -> none  [turn(): return total.at[target].add(masked)]
    dot_general x7 -> x0, matrix products: 22.5 us -> none  [the longest x2 9.17 us: turn(): jnp.einsum('tvc,tvw->tcw', vals, picked, preferred_element_type=jnp.float32)]
    while x1 -> x0, local copies, waits for them, and re-layouts: 12 us -> none  [accumulate(): return lax.fori_loop(0, blocks, turn, init)]
    gather x4 -> x0, local copies, waits for them, and re-layouts: 11.3 us -> none  [the longest x2 7.16 us: turn(): picked = panels[rws]]
  transfers between devices with their start and end apart: 9 -> 0, of which waited for: 9 -> 0; matrix products, arithmetic and copies ran while one was open for 10% -> 0% of each run, Pallas kernels for 0% -> 0%
where the time goes in v2:
time: 98.3 us; the launch traced here: 97 us
  Pallas kernels  95.7 us (97%)
  between operations  1.29 us (1%)
    pallas_call x1, Pallas kernels, shards(): pl.pallas_call(body, out_shape=(jax.ShapeDtypeStruct((2 * T, F), F32), ja...  91.5 us
    pallas_call x1, Pallas kernels, shards(): pl.pallas_call(tail, out_shape=(jax.ShapeDtypeStruct((2 * T, F), BF), jax...  2.19 us
    pallas_call x1, Pallas kernels, shards(): pl.pallas_call(order_tiles, out_shape=(table, table), in_specs=[smem, vme...  2.08 us

profile of v2, /device:TPU:0, one launch (start us, length us, event | category | flops | bytes accessed | tf_op | source)
XLA Modules:
  0.0 97.0 jit_solution(9197485876802397592)
XLA Ops:
  1.3 2.1 %shard_map.129 = (s32[8,384]{1,0:T(8,128)}, s32[8,384]{1,0:T(8,128)}) custom-call(s32[1]{0:T(128)S(6)} %copy.14.count_ref, s32[1,256]{1,0:T(1,128)} %bitcast.3, s32[1,256]{1,0:T(1,128)} %bitcast.4), custom_call_target="tpu_custom_call" | custom-call | flops 1000000 | bytes 30000 | tf_op jit(solution)/shard_map/pallas_call | solution.py:505
  3.4 91.5 %shard_map.130 = (f32[256,256]{1,0:T(8,128)}, bf16[256,256]{1,0:T(8,128)(2,1)}, f32[256,256]{1,0:T(8,128)}, f32[1,384]{1,0:T(1,128)}) custom-call(s32[8,384]{1,0:T(8,128)} %get-tuple-element.10.by_col, s32[8,384]{1,0:T(8,128)} %get-tuple-element.11.by_row, bf16[256,256]{1,0:T(8,128)(2,1)} %x_ref.1, bf16[256,256]{1,0:T(8,128)(2,1)} %g_ref.1, ...), custom_call_target="tpu_custom_call" | custom-call | flops 20000000000 | bytes 10000000 | tf_op jit(solution)/shard_map/pallas_call | solution.py:512
  94.8 2.2 %shard_map.131 = (bf16[256,256]{1,0:T(8,128)(2,1)}, bf16[256,256]{1,0:T(8,128)(2,1)}, f32[256,256]{1,0:T(8,128)}, f32[1,384]{1,0:T(1,128)}) custom-call(f32[256,256]{1,0:T(8,128)} %get-tuple-element.12.ys_ref, bf16[256,256]{1,0:T(8,128)(2,1)} %get-tuple-element.13.gz_ref, f32[256,256]{1,0:T(8,128)} %get-tuple-element.14.gt_ref, ...), custom_call_target="tpu_custom_call" | custom-call | flops 100000000 | bytes 2000000 | tf_op jit(solution)/shard_map/pallas_call | solution.py:533

commit v3 on v2

--- a/solution.py
+++ b/solution.py
@@ -17,7 +17,7 @@
 GB = (SLOTS + VB) // 2
 PARTS = 2
 NSEND = 29
-NRECV = 57
+NRECV = 69
 
 
 def plan(key, other, live, pad):
@@ -66,7 +66,7 @@
     y_ref, gz_ref, gt_ref, gw_ref,
     tiles, run, scale, theta_t,
     pt_0, pt_1, pt_2, pt_3, e_0, e_1, e_2, e_3,
-    sib_s, sib_r, mine, zs, zr, bxt, bgt, vs, vr, vkeep, ws, wr,
+    sib_s, sib_r, mine, zs, zr, bxt, bgt, vs, vr1, vr2, vkeep, ws, wr,
     gl, g1, gp1, g2, g3, go,
     tsem, ssem, rsem,
 ):
@@ -134,24 +134,41 @@
         def to(h, a, b):
             return xy(b, a) if h == 0 else xy(a, b)
 
-        out, one, two = leaving(pt.at[pl.ds(0, 30)]), coming(), coming()
-        own = [pt.at[2 * j + h] for h in range(2)]
+        def block(h, a, b):
+            dx, dy = (b, a) if h == 0 else (a, b)
+            return pt.at[2 * (((x + dx) % 4) * 4 + (y + dy) % 4) + h]
+
+        out = leaving(pt.at[pl.ds(0, 30)])
+        one, two, three, four = [coming() for _ in range(4)]
         for d in near:
             for h in range(2):
-                send(own[h], own[h], to(h, d, 0), out, one)
-        for d in near:
-            for h in range(2):
-                send(own[h], own[h], to(h, 0, d), out, two)
+                send(block(h, 0, 0), block(h, 0, 0), to(h, d, 0), out, one)
+
+        def across(a, into):
+            for d in (1, -1):
+                for h in range(2):
+                    send(block(h, a, 0), block(h, a, 0), to(h, 0, d), out, into)
+
+        def onward(a):
+            for d, start in ((1, 0), (-1, T // 2)):
+                for h in range(2):
+                    r = block(h, a, -d).at[pl.ds(start, T // 2)]
+                    send(r, r, to(h, 0, d), out, four)
+
+        across(0, two)
         yield
         arrived(pt.at[pl.ds(0, 6)], one)
         for a in near:
-            for d in near:
-                for h in range(2):
-                    dx, dy = (0, a) if h == 0 else (a, 0)
-                    r = pt.at[2 * (((x + dx) % 4) * 4 + (y + dy) % 4) + h]
-                    send(r, r, to(h, 0, d), out, two)
-        yield
-        arrived(pt.at[pl.ds(0, 24)], two)
+            across(a, three)
+        yield
+        arrived(pt.at[pl.ds(0, 4)], two)
+        onward(0)
+        yield
+        arrived(pt.at[pl.ds(0, 12)], three)
+        for a in near:
+            onward(a)
+        yield
+        arrived(pt.at[pl.ds(0, 8)], four)
 
     def sweep(table, groups, unit, part, product):
         per = groups // PARTS
@@ -272,31 +289,58 @@
             dx, dy = (p, q) if h == 0 else (q, p)
             return run[by_row[3, 2 * (((x + dx) % 4) * 4 + (y + dy) % 4) + h]]
 
-        out, out2, one, two = leaving(vs.at[k]), leaving(ws.at[k]), coming(), coming()
-        for p in near:
-            for h in range(2):
-                for q in range(4):
-                    vs[k, h, p - 1, q] = fetch(h, p, q).astype(BF)
-                send(vs.at[k, h, p - 1], vr.at[k, h, p - 1], to(h, p, 0), out, one)
+        out, out2 = leaving(vs.at[k]), leaving(ws.at[k])
+        one, two, three = [coming() for _ in range(3)]
+
+        def halves(v):
+            return v[: T // 2], v[T // 2 :]
+
         for h in range(2):
             for q in range(4):
-                vkeep[k, h, q] = fetch(h, 0, q)
-        yield
-        arrived(vr.at[k], one)
+                for u, v in enumerate(halves(fetch(h, 2, q))):
+                    vs[k, h, 0, u, q] = v.astype(BF)
+            for u, d in ((0, 1), (1, -1)):
+                send(vs.at[k, h, 0, u], vr1.at[k, h, u], to(h, d, 0), out, one)
+        for h in range(2):
+            for q in range(4):
+                up, down = halves(fetch(h, 1, q))
+                vs[k, h, 1, 1, q] = down.astype(BF)
+                vkeep[k, h, 1, q, : T // 2] = up
+                up, down = halves(fetch(h, 3, q))
+                vs[k, h, 2, 0, q] = up.astype(BF)
+                vkeep[k, h, 1, q, T // 2 :] = down
+            send(vs.at[k, h, 1, 1], vr2.at[k, h, 0, 1], to(h, 1, 0), out, two)
+            send(vs.at[k, h, 2, 0], vr2.at[k, h, 1, 0], to(h, -1, 0), out, two)
+        for h in range(2):
+            for q in range(4):
+                vkeep[k, h, 0, q] = fetch(h, 0, q)
+        yield
+        arrived(vr1.at[k], one)
+        for h in range(2):
+            for q in range(4):
+                up, down = halves(vkeep[k, h, 1, q])
+                vs[k, h, 1, 0, q] = (up + vr1[k, h, 0, q].astype(F32)).astype(BF)
+                vs[k, h, 2, 1, q] = (down + vr1[k, h, 1, q].astype(F32)).astype(BF)
+            send(vs.at[k, h, 1, 0], vr2.at[k, h, 0, 0], to(h, 1, 0), out, two)
+            send(vs.at[k, h, 2, 1], vr2.at[k, h, 1, 1], to(h, -1, 0), out, two)
+        yield
+        arrived(vr2.at[k], two)
         for q in (1, 3, 2, 0):
             for h in range(2):
-                total = vkeep[k, h, q]
-                for p in range(3):
-                    total = total + vr[k, h, p, q].astype(F32)
+                total = vkeep[k, h, 0, q]
+                for p in range(2):
+                    total = total + jnp.concatenate(
+                        [vr2[k, h, p, u, q].astype(F32) for u in range(2)], axis=0
+                    )
                 if q:
                     ws[k, h, q - 1] = total.astype(BF)
-                    send(ws.at[k, h, q - 1], wr.at[k, h, q - 1], to(h, 0, q), out2, two)
+                    send(ws.at[k, h, q - 1], wr.at[k, h, q - 1], to(h, 0, q), out2, three)
                 else:
-                    vkeep[k, h, 0] = total
-        yield
-        arrived(wr.at[k], two)
+                    vkeep[k, h, 0, 0] = total
+        yield
+        arrived(wr.at[k], three)
         for h in range(2):
-            v = vkeep[k, h, 0]
+            v = vkeep[k, h, 0, 0]
             for q in range(3):
                 v = v + wr[k, h, q].astype(F32)
             rows = pl.ds(h * T, T)
@@ -370,42 +414,50 @@
         run[0] = jnp.zeros((T, T), F32)
 
     step(row[0])
+    step(row[0])
+    step(row[0])
     step(row[1])
     prepare(g_ref, 2)
-    step(row[2])
     tables()
-    step(row[3])
     step(row[0])
     step(row[1])
+    step(row[1])
     step(row[2])
-    step(row[3])
     step(row[0])
     load.wait()
     forward(0, 0)
     forward(0, 1)
     step(col[0])
     step(row[1])
+    step(col[0])
+    step(row[2])
+    step(row[2])
+    step(row[3])
+    step(row[1])
     forward(1, 0)
-    step(col[0])
     forward(1, 1)
     step(col[1])
     step(row[2])
+    step(col[0])
+    step(col[1])
+    step(full[0])
+    step(row[3])
+    step(row[3])
+    step(row[2])
     forward(2, 0)
-    step(col[1])
     forward(2, 1)
     step(col[2])
     step(row[3])
+    step(col[1])
+    step(col[2])
+    step(full[1])
+    step(row[3])
     forward(3, 0)
-    step(col[0])
-    step(full[0])
-    step(col[2])
     forward(3, 1)
-    step(col[3])
-    step(col[1])
-    step(full[1])
     step(col[3])
     step(full[0])
     step(full[0])
+    step(col[3])
     step(full[0])
     backward(0, 0)
     backward(0, 1)
@@ -416,30 +468,32 @@
     step(full[1])
     step(full[1])
     backward(1, 0)
-    backward(1, 1)
+    step(back[0])
     step(col[3])
     step(theta)
+    step(full[3])
+    backward(1, 1)
+    step(back[1])
     step(back[0])
-    step(back[1])
-    weights_grad()
-    step(full[3])
     step(full[2])
     step(full[2])
+    weights_grad()
     step(full[2])
     backward(2, 0)
+    step(theta)
+    step(back[1])
+    backward(2, 1)
+    step(back[2])
+    step(theta)
     step(back[0])
-    backward(2, 1)
-    step(theta)
-    step(back[2])
     step(full[3])
     step(full[3])
-    step(theta)
     step(back[1])
     step(full[3])
     backward(3, 0)
     backward(3, 1)
+    step(theta)
     step(back[3])
-    step(theta)
     step(back[2])
     step(back[1])
     step(theta)
@@ -447,6 +501,8 @@
     step(back[2])
     step(back[3])
     step(theta)
+    step(back[2])
+    step(back[3])
     for ref, n in sends:
         pltpu.make_async_copy(ref, ref, ssem.at[n]).wait()
 
@@ -486,9 +542,10 @@
         v((4, 3, 3, T, T), BF),
         v((2, 3, T, T), F32),
         v((2, 3, T, T), F32),
-        v((4, 2, 3, 4, T, T), BF),
-        v((4, 2, 3, 4, T, T), BF),
-        v((4, 2, 4, T, T), F32),
+        v((4, 2, 3, 2, 4, T // 2, T), BF),
+        v((4, 2, 2, 4, T // 2, T), BF),
+        v((4, 2, 2, 2, 4, T // 2, T), BF),
+        v((4, 2, 2, 4, T, T), F32),
         v((4, 2, 3, T, T), BF),
         v((4, 2, 3, T, T), BF),
         v((F, F), F32),

time: 98.3 us -> 92.6 us (0.942)
  Pallas kernels: 95.7 us -> 90.9 us
    pallas_call x1, Pallas kernels: 91.5 us -> 86.6 us  [shards(): pl.pallas_call(body, out_shape=(jax.ShapeDtypeStruct((2 * T, F), F32), ja...]
where the time goes in v3:
time: 92.6 us; the launch traced here: 92.1 us
  Pallas kernels  90.9 us (98%)
  between operations  1.29 us (1%)
    pallas_call x1, Pallas kernels, shards(): pl.pallas_call(body, out_shape=(jax.ShapeDtypeStruct((2 * T, F), F32), ja...  86.6 us
    pallas_call x1, Pallas kernels, shards(): pl.pallas_call(tail, out_shape=(jax.ShapeDtypeStruct((2 * T, F), BF), jax...  2.18 us
    pallas_call x1, Pallas kernels, shards(): pl.pallas_call(order_tiles, out_shape=(table, table), in_specs=[smem, vme...  2.08 us

profile of v3, /device:TPU:0, one launch (start us, length us, event | category | flops | bytes accessed | tf_op | source)
XLA Modules:
  0.0 92.1 jit_solution(1377066923965082664)
XLA Ops:
  1.3 2.1 %shard_map.129 = (s32[8,384]{1,0:T(8,128)}, s32[8,384]{1,0:T(8,128)}) custom-call(s32[1]{0:T(128)S(6)} %copy.14.count_ref, s32[1,256]{1,0:T(1,128)} %bitcast.3, s32[1,256]{1,0:T(1,128)} %bitcast.4), custom_call_target="tpu_custom_call" | custom-call | flops 1000000 | bytes 30000 | tf_op jit(solution)/shard_map/pallas_call | solution.py:562
  3.4 86.6 %shard_map.130 = (f32[256,256]{1,0:T(8,128)}, bf16[256,256]{1,0:T(8,128)(2,1)}, f32[256,256]{1,0:T(8,128)}, f32[1,384]{1,0:T(1,128)}) custom-call(s32[8,384]{1,0:T(8,128)} %get-tuple-element.10.by_col, s32[8,384]{1,0:T(8,128)} %get-tuple-element.11.by_row, bf16[256,256]{1,0:T(8,128)(2,1)} %x_ref.1, bf16[256,256]{1,0:T(8,128)(2,1)} %g_ref.1, ...), custom_call_target="tpu_custom_call" | custom-call | flops 20000000000 | bytes 10000000 | tf_op jit(solution)/shard_map/pallas_call | solution.py:569
  90.0 2.2 %shard_map.131 = (bf16[256,256]{1,0:T(8,128)(2,1)}, bf16[256,256]{1,0:T(8,128)(2,1)}, f32[256,256]{1,0:T(8,128)}, f32[1,384]{1,0:T(1,128)}) custom-call(f32[256,256]{1,0:T(8,128)} %get-tuple-element.12.ys_ref, bf16[256,256]{1,0:T(8,128)(2,1)} %get-tuple-element.13.gz_ref, f32[256,256]{1,0:T(8,128)} %get-tuple-element.14.gt_ref, ...), custom_call_target="tpu_custom_call" | custom-call | flops 100000000 | bytes 2000000 | tf_op jit(solution)/shard_map/pallas_call | solution.py:590

commit v4 on v3

--- a/solution.py
+++ b/solution.py
@@ -24,51 +24,42 @@
     n = SLOTS
 
     def iota(shape, dim):
-        return lax.broadcasted_iota(jnp.int32, shape, dim).astype(F32)
-
-    key_l = jnp.broadcast_to(key.astype(F32), (n, n))
-    key_l = jnp.where(iota((n, n), 1) < live, key_l, float(n))
+        return lax.broadcasted_iota(jnp.int32, shape, dim)
+
+    key_l = jnp.where(iota((n, n), 1) < live, jnp.broadcast_to(key, (n, n)), n)
     key_s = jnp.transpose(key_l)
-    other_s = jnp.transpose(jnp.broadcast_to(other.astype(F32), (n, n)))
+    other_s = jnp.transpose(jnp.broadcast_to(other, (n, n)))
     t = iota((n, n), 0)
-    same = jnp.where((key_s == key_l) & (iota((n, n), 1) < t), 1.0, 0.0)
+    same = jnp.where((key_s == key_l) & (iota((n, n), 1) < t), 1, 0)
     rank = jnp.sum(same, axis=1, keepdims=True)
-    hit = jnp.where(key_s[:, :T] == iota((n, T), 1), 1.0, 0.0)
+    hit = jnp.where(key_s[:, :T] == iota((n, T), 1), 1, 0)
     count = jnp.sum(hit, axis=0, keepdims=True)
-    half = jnp.floor((count + 1.0) * 0.5)
-    upto = jnp.where(iota((T, T), 0) <= iota((T, T), 1), 1.0, 0.0)
-    end = jnp.dot(
-        jnp.broadcast_to(half, (8, T)).astype(BF), upto.astype(BF), preferred_element_type=F32
-    )[:1]
-    start = 2.0 * (end - half)
+    half = (count + 1) >> 1
+    upto = iota((T, T), 0) <= iota((T, T), 1)
+    half_s = jnp.transpose(jnp.broadcast_to(half, (T, T)))
+    end = jnp.sum(jnp.where(upto, half_s, 0), axis=0, keepdims=True)
+    start = 2 * (end - half)
     place = jnp.sum(hit * start, axis=1, keepdims=True) + rank
-    place = jnp.where(key_s[:, :1] < float(n), place, -1.0)
-    at = jnp.where(place == iota((n, pad), 1), 1.0, 0.0)
-    tile = jnp.sum(at * (t[:, :1] - float(n)), axis=0, keepdims=True) + float(n)
-    panel = jnp.sum(at * other_s[:, :1], axis=0, keepdims=True)
-    more = jnp.where(rank > 0.0, 1.0, 0.0)
-    keep = jnp.sum(jnp.where(place == 2.0 * iota((n, pad), 1), more, 0.0), axis=0, keepdims=True)
-    last = jnp.where(count > 0.0, end, 0.0)
-    last = jnp.concatenate([last, jnp.zeros((1, pad - T), F32)], axis=1)
-    rows = jnp.concatenate([tile, panel, keep, last, jnp.zeros((4, pad), F32)], axis=0)
-    return rows.astype(jnp.int32)
-
-
-def order_tiles(count_ref, rows_ref, cols_ref, by_col, by_row):
-    live = count_ref[0].astype(F32)
-    by_col[...] = plan(cols_ref[...], rows_ref[...], live, 384)
-    by_row[...] = plan(rows_ref[...], cols_ref[...], live, 384)
+    place = jnp.where(key_s[:, :1] < n, place, -1)
+    at = place == iota((n, pad), 1)
+    tile = jnp.sum(jnp.where(at, t[:, :1] - n, 0), axis=0, keepdims=True) + n
+    panel = jnp.sum(jnp.where(at, other_s[:, :1], 0), axis=0, keepdims=True)
+    more = jnp.where(rank > 0, 1, 0)
+    keep = jnp.sum(jnp.where(place == 2 * iota((n, pad), 1), more, 0), axis=0, keepdims=True)
+    last = jnp.where(count > 0, end, 0)
+    last = jnp.concatenate([last, jnp.zeros((1, pad - T), jnp.int32)], axis=1)
+    return jnp.concatenate([tile, panel, keep, last, jnp.zeros((4, pad), jnp.int32)], axis=0)
 
 
 def body(
-    by_col, by_row,
+    count_ref, rows_ref, cols_ref,
     x_ref, g_ref, theta_ref, values_ref, vdeg_ref, ew_ref, ed_ref,
     y_ref, gz_ref, gt_ref, gw_ref,
-    tiles, run, scale, theta_t,
+    tiles, run, scale, theta_t, plans, by_col, by_row,
     pt_0, pt_1, pt_2, pt_3, e_0, e_1, e_2, e_3,
     sib_s, sib_r, mine, zs, zr, bxt, bgt, vs, vr1, vr2, vkeep, ws, wr,
     gl, g1, gp1, g2, g3, go,
-    tsem, ssem, rsem,
+    tsem, psem, ssem, rsem,
 ):
     pts, es = (pt_0, pt_1, pt_2, pt_3), (e_0, e_1, e_2, e_3)
     i = lax.axis_index("vrow")
@@ -408,7 +399,17 @@
     full = [gather_col(k) for k in range(4)]
     back = [reduce_row(k) for k in range(4)]
     theta = sum_theta()
+    copies = [
+        pltpu.make_async_copy(plans.at[m], dst, psem.at[m])
+        for m, dst in enumerate((by_col, by_row))
+    ]
+
     def tables():
+        live = count_ref[0]
+        plans[0] = plan(cols_ref[...], rows_ref[...], live, 384)
+        plans[1] = plan(rows_ref[...], cols_ref[...], live, 384)
+        for c in copies:
+            c.start()
         theta_t[...] = jnp.transpose(theta_ref[...].astype(F32)).astype(BF)
         tiles[SLOTS] = jnp.zeros((T, T), BF)
         run[0] = jnp.zeros((T, T), F32)
@@ -425,6 +426,8 @@
     step(row[2])
     step(row[0])
     load.wait()
+    for c in copies:
+        c.wait()
     forward(0, 0)
     forward(0, 1)
     step(col[0])
@@ -533,6 +536,9 @@
         v((GB + 1, T, T), F32),
         v((2 * T, F), F32),
         v((F, F), BF),
+        v((2, 8, 384), jnp.int32),
+        pltpu.SMEM((8, 384), jnp.int32),
+        pltpu.SMEM((8, 384), jnp.int32),
         *[v((VB, T, T), BF)] * 4,
         *[v((EB, T, T), BF)] * 4,
         v((4, 4, 3, T, T), BF),
@@ -555,17 +561,10 @@
         v((4, 8, F), F32),
         v((F, F), F32),
         pltpu.SemaphoreType.DMA,
+        pltpu.SemaphoreType.DMA((2,)),
         pltpu.SemaphoreType.DMA((NSEND,)),
         pltpu.SemaphoreType.DMA((NRECV,)),
     ]
-    table = jax.ShapeDtypeStruct((8, 384), jnp.int32)
-    by_col, by_row = pl.pallas_call(
-        order_tiles,
-        out_shape=(table, table),
-        in_specs=[smem, vmem, vmem],
-        out_specs=[vmem] * 2,
-        cost_estimate=pl.CostEstimate(flops=1_000_000, bytes_accessed=30_000, transcendentals=0),
-    )(tile_count, tile_rows.reshape(1, SLOTS), tile_cols.reshape(1, SLOTS))
     ys, gz, gt, gw = pl.pallas_call(
         body,
         out_shape=(
@@ -574,7 +573,7 @@
             jax.ShapeDtypeStruct((F, F), F32),
             jax.ShapeDtypeStruct((1, 3 * T), F32),
         ),
-        in_specs=[smem] * 2 + [vmem] * 3 + [hbm] + [vmem] * 3,
+        in_specs=[smem] + [vmem] * 5 + [hbm] + [vmem] * 3,
         out_specs=[vmem] * 4,
         scratch_shapes=scratch,
         compiler_params=pltpu.CompilerParams(
@@ -584,8 +583,8 @@
             flops=20_000_000_000, bytes_accessed=10_000_000, transcendentals=0
         ),
     )(
-        by_col, by_row, features, grad_out, theta, tile_values, vertex_degree.reshape(1, 2 * T),
-        edge_weight, edge_degree,
+        tile_count, tile_rows.reshape(1, SLOTS), tile_cols.reshape(1, SLOTS), features, grad_out,
+        theta, tile_values, vertex_degree.reshape(1, 2 * T), edge_weight, edge_degree,
     )
     return pl.pallas_call(
         tail,

time: 92.6 us -> 90.6 us (0.978)
  Pallas kernels: 90.9 us -> 88.8 us
    pallas_call x1 -> x0, Pallas kernels: 2.08 us -> none  [shards(): pl.pallas_call(order_tiles, out_shape=(table, table), in_specs=[smem, vme...]
where the time goes in v4:
time: 90.6 us; the launch traced here: 90.1 us
  Pallas kernels  88.8 us (98%)
  between operations  1.29 us (1%)
    pallas_call x1, Pallas kernels, shards(): pl.pallas_call(body, out_shape=(jax.ShapeDtypeStruct((2 * T, F), F32), ja...  86.6 us
    pallas_call x1, Pallas kernels, shards(): pl.pallas_call(tail, out_shape=(jax.ShapeDtypeStruct((2 * T, F), BF), jax...  2.19 us

profile of v4, /device:TPU:0, one launch (start us, length us, event | category | flops | bytes accessed | tf_op | source)
XLA Modules:
  0.0 90.1 jit_solution(5266264357692952624)
XLA Ops:
  1.3 86.6 %shard_map.129 = (f32[256,256]{1,0:T(8,128)}, bf16[256,256]{1,0:T(8,128)(2,1)}, f32[256,256]{1,0:T(8,128)}, f32[1,384]{1,0:T(1,128)}) custom-call(s32[1]{0:T(128)S(6)} %copy.14.count_ref, s32[1,256]{1,0:T(1,128)} %bitcast.3, s32[1,256]{1,0:T(1,128)} %bitcast.4, bf16[256,256]{1,0:T(8,128)(2,1)} %x_ref.1, bf16[256,256]{1,0:T(8,128)(2,1)} %g_ref.1, ...), custom_call_target="tpu_custom_call" | custom-call | flops 20000000000 | bytes 10000000 | tf_op jit(solution)/shard_map/pallas_call | solution.py:568
  87.9 2.2 %shard_map.130 = (bf16[256,256]{1,0:T(8,128)(2,1)}, bf16[256,256]{1,0:T(8,128)(2,1)}, f32[256,256]{1,0:T(8,128)}, f32[1,384]{1,0:T(1,128)}) custom-call(f32[256,256]{1,0:T(8,128)} %get-tuple-element.8.ys_ref, bf16[256,256]{1,0:T(8,128)(2,1)} %get-tuple-element.9.gz_ref, f32[256,256]{1,0:T(8,128)} %get-tuple-element.10.gt_ref, ...), custom_call_target="tpu_custom_call" | custom-call | flops 100000000 | bytes 2000000 | tf_op jit(solution)/shard_map/pallas_call | solution.py:589
